TPU v7x, 32 devices: a whole 2x2x4 slice. The times are simulated.
32 devices in a mesh: rows: 8 (over y, x, core), labels: 4 (over z).
Axes of the slice: x: 2, y: 2, z: 4, core: 2. Of those that a mesh axis runs over, the one named last changes fastest.
Arguments:
- points: bfloat16 [4096, 1024], P('rows'), may hold values from -6 to 6
- targets: bfloat16 [4096, 21504], P('rows', 'labels'), may hold values from -6 to 6
- coeffs: float32 [4096, 21504], P('rows', 'labels'), may hold values from -6 to 6
- block_ids: int32 [2, 512], replicated, may hold values from 0 to 4095, as said below
- inverses: float32 [2, 512, 512], replicated, as said below
Outputs:
- new_coeffs: float32 [4096, 21504], P('rows', 'labels')
Inputs may be any that keep to these rules, and one draw needn't show every extreme that they name: `block_ids`: the 512 ids of one block are distinct; the two blocks may share ids. Each inverses[b] is symmetric with a positive diagonal.
All inputs are finite; a program needn't handle non-finite values.
Results may differ from a plain program's by a relative error of at most 0.0029.
Values may be sent and summed in bfloat16 or wider, within the bound.
No kernel may reach another device: no remote copies, remote signals or barrier semaphores. Data moves between devices by JAX's collectives and lax.ppermute only.
A program may use at most 128 MiB of HBM per device.

v0:
```python
import jax
import jax.numpy as jnp
from jax import lax
from jax.sharding import PartitionSpec as P

ridge_weight = 0.5


def kernel_tile(left, right):
    inner_prod = lax.dot_general(
        left, right, (((1,), (1,)), ((), ())), preferred_element_type=jnp.float32
    )
    left_sq = jnp.sum(jnp.square(left.astype(jnp.float32)), axis=1)
    right_sq = jnp.sum(jnp.square(right.astype(jnp.float32)), axis=1)
    sq_dist = jnp.maximum(left_sq[:, None] + right_sq[None, :] - 2.0 * inner_prod, 0.0)
    return jnp.exp(-(2.0 / left.shape[1]) * sq_dist).astype(jnp.bfloat16)


def per_device(points, targets, coeffs, block_ids, inverses):
    rows_here = points.shape[0]
    first_row = lax.axis_index("rows") * rows_here
    zero_low = jnp.zeros((), jnp.bfloat16)
    current = coeffs
    for blk in range(2):
        local_ids = block_ids[blk] - first_row
        inside = (local_ids >= 0) & (local_ids < rows_here)
        inside, local_rows = (inside, jnp.clip(local_ids, 0, rows_here - 1))
        picked = jnp.where(inside[:, None], points[local_rows], zero_low)
        block_pts = lax.psum(picked, "rows").astype(jnp.float32).astype(jnp.bfloat16)
        ktile = kernel_tile(points, block_pts)
        c_low = current.astype(jnp.bfloat16)
        sel_targets = jnp.where(inside[:, None], targets[local_rows].astype(jnp.float32), 0.0)
        sel_coeffs = jnp.where(inside[:, None], current[local_rows], 0.0)
        local_side = ridge_weight * sel_coeffs - sel_targets
        product = lax.dot_general(
            ktile, c_low, (((0,), (0,)), ((), ())), preferred_element_type=jnp.float32
        )
        share = lax.psum_scatter(product + local_side, "rows", scatter_dimension=0, tiled=True)
        negated = lax.all_gather(share, "rows", axis=0, tiled=True)
        update = jnp.dot(
            inverses[blk],
            -negated,
            precision=lax.Precision.HIGHEST,
            preferred_element_type=jnp.float32,
        )
        current = current.at[local_rows].add(jnp.where(inside[:, None], update, 0.0))
    return current


def solution(mesh):
    return jax.shard_map(
        per_device,
        mesh=mesh,
        in_specs=(P("rows", None), P("rows", "labels"), P("rows", "labels"), P(), P()),
        out_specs=P("rows", "labels"),
        check_vma=False,
    )
```

profile of v0, /device:TPU:0, one launch (start us, length us, event | category | flops | bytes accessed | tf_op | source)
XLA Modules:
  0.0 597.6 jit_solution(10181298061620878957)
XLA Ops:
  6.5 9.2 %copy.15 = f32[512,5376]{1,0:T(8,128)} copy(f32[512,5376]{1,0:T(8,128)} %param.7) | data formatting | bytes 22020096
  15.8 0.5 copy-done.5
  16.4 2.1 gather_fusion
  18.4 2.1 gather_fusion.3
  20.5 1.6 broadcast_select_fusion
  22.3 15.4 %gather_fusion.1 = f32[512,5376]{1,0:T(8,128)} fusion(f32[512,5376]{1,0:T(8,128)} %copy.15, s32[1024]{0:T(1024)S(1)} %pad_clamp_fusion.1), kind=kCustom, calls=%fused_computation.1 | custom fusion | bytes 22022144 | tf_op jit(solution)/shard_map/gather | solution.py:33
  37.7 14.2 %gather_fusion.2 = bf16[512,5376]{1,0:T(8,128)(2,1)} fusion(bf16[512,5376]{1,0:T(8,128)(2,1)} %param.6, s32[1024]{0:T(1024)S(1)} %pad_clamp_fusion.1), kind=kCustom, calls=%fused_computation.2 | custom fusion | bytes 11012096 | tf_op jit(solution)/shard_map/gather | solution.py:32
  52.0 0.3 multiply_reduce_fusion.2
  52.3 34.2 %all-reduce.3.cloned.1.call-done = (bf16[512,1024]{1,0:T(8,128)(2,1)}, bf16[512,1024]{1,0:T(8,128)(2,1)}) async-done(((bf16[512,1024]{1,0:T(8,128)(2,1)}, bf16[512,1024]{1,0:T(8,128)(2,1)}), (bf16[512,1024]{1,0:T(8,128)(2,1)}, bf16[512,1024]{1,0:T(8,128)(2,1)})) %all-reduce.3.cloned.1.call-update) | async-done | bytes 2097168 | tf_op jit(solution)/shard_map/psum | solution.py:29
  86.5 1.5 multiply_reduce_fusion.1
  88.0 16.2 %subtract_add_fusion.1 = f32[512,5376]{1,0:T(8,128)} fusion(bf16[512,5376]{1,0:T(8,128)(2,1)} %gather_fusion.2, f32[512,5376]{1,0:T(8,128)} %gather_fusion.1, f32[512,5376]{1,0:T(8,128)} %copy.15, pred[512]{0:T(512)(128)(4,1)S(1)} %get-tuple-element.6, bf16[512,1024]{1,0:T(8,128)(2,1)} %get-tuple-element.7, bf16[512,1024]{1,0:T(8,128)(2,1)S(1)} %copy-done, ...), kind=kOutput, calls=%fused_computation.15 | convolution fusion | flops 3376283648 | bytes 40636928 | tf_op jit(solution)/shard_map/dot_general | solution.py:35
  104.3 83.3 %reduce-scatter.3.cloned.1.call-done = f32[64,5376]{1,0:T(8,128)} async-done(((f32[512,5376]{1,0:T(8,128)}), f32[64,5376]{1,0:T(8,128)}) %reduce-scatter.3.cloned.1.call-update) | async-done | bytes 1376272 | tf_op jit(solution)/shard_map/reduce_scatter | solution.py:38
  187.7 14.3 %gather_fusion.5 = bf16[512,5376]{1,0:T(8,128)(2,1)} fusion(bf16[512,5376]{1,0:T(8,128)(2,1)} %param.6, s32[1024]{0:T(1024)S(1)} %pad_clamp_fusion), kind=kCustom, calls=%fused_computation.5 | custom fusion | bytes 11012096 | tf_op jit(solution)/shard_map/gather | solution.py:32
  202.3 52.7 %all-gather.3.cloned.1.call-done = f32[512,5376]{1,0:T(8,128)} async-done(((f32[64,5376]{1,0:T(8,128)}), f32[512,5376]{1,0:T(8,128)}) %all-gather.3.cloned.1.call-update) | async-done | bytes 11010064 | tf_op jit(solution)/shard_map/all_gather | solution.py:39
  255.0 39.3 %select_bitcast_fusion.1 = f32[512,5376]{0,1:T(8,128)} fusion(f32[512,5376]{1,0:T(8,128)} %all-gather.3.cloned.1.call-done, pred[512]{0:T(512)(128)(4,1)S(1)} %get-tuple-element.6, f32[2,512,512]{2,1,0:T(8,128)} %param.9), kind=kOutput, calls=%fused_computation.12 | convolution fusion | flops 16916938752 | bytes 23069184 | tf_op jit(solution)/shard_map/dot_general | solution.py:40
  294.3 12.1 %copy.8 = f32[512,5376]{1,0:T(8,128)} copy(f32[512,5376]{0,1:T(8,128)} %select_bitcast_fusion.1) | data formatting | bytes 22020096 | tf_op jit(solution)/shard_map/jit(_where)/select_n | solution.py:46
  306.4 25.8 %scatter_fusion = f32[512,5376]{1,0:T(8,128)} fusion(f32[512,5376]{1,0:T(8,128)} %copy.15, s32[512]{0:T(512)S(1)} %bitcast.51, f32[512,5376]{1,0:T(8,128)} %copy.8), kind=kCustom, calls=%fused_computation.6 | custom fusion | flops 2752512 | bytes 33032192 | tf_op jit(solution)/shard_map/scatter-add | solution.py:46
  332.2 15.4 %gather_fusion.4 = f32[512,5376]{1,0:T(8,128)} fusion(f32[512,5376]{1,0:T(8,128)} %scatter_fusion, s32[1024]{0:T(1024)S(1)} %pad_clamp_fusion), kind=kCustom, calls=%fused_computation.4 | custom fusion | bytes 22022144 | tf_op jit(solution)/shard_map/gather | solution.py:33
  347.6 15.0 %subtract_add_fusion = f32[512,5376]{1,0:T(8,128)} fusion(bf16[512,5376]{1,0:T(8,128)(2,1)} %gather_fusion.5, f32[512,5376]{1,0:T(8,128)} %gather_fusion.4, f32[512,5376]{1,0:T(8,128)} %scatter_fusion, pred[512]{0:T(512)(128)(4,1)S(1)} %copy-done.4, bf16[512,1024]{1,0:T(8,128)(2,1)S(1)} %copy-done.1, bf16[512,1024]{1,0:T(8,128)(2,1)S(1)} %copy-done, ...), kind=kOutput, calls=%fused_computation.11 | convolution fusion | flops 3376283648 | bytes 40636928 | tf_op jit(solution)/shard_map/dot_general | solution.py:35
  362.8 84.1 %reduce-scatter.5.cloned.1.call-done = f32[64,5376]{1,0:T(8,128)} async-done(((f32[512,5376]{1,0:T(8,128)}), f32[64,5376]{1,0:T(8,128)}) %reduce-scatter.5.cloned.1.call-update) | async-done | bytes 1376272 | tf_op jit(solution)/shard_map/reduce_scatter | solution.py:38
  446.9 67.2 %all-gather.5.cloned.1.call-done = f32[512,5376]{1,0:T(8,128)} async-done(((f32[64,5376]{1,0:T(8,128)}), f32[512,5376]{1,0:T(8,128)}) %all-gather.5.cloned.1.call-update) | async-done | bytes 11010064 | tf_op jit(solution)/shard_map/all_gather | solution.py:39
  514.1 39.0 %select_bitcast_fusion = f32[512,5376]{0,1:T(8,128)} fusion(f32[512,5376]{1,0:T(8,128)} %all-gather.5.cloned.1.call-done, pred[512]{0:T(512)(128)(4,1)S(1)} %copy-done.4, f32[2,512,512]{2,1,0:T(8,128)S(1)} %copy-done.2), kind=kOutput, calls=%fused_computation.8 | convolution fusion | flops 16916938752 | bytes 23069184 | tf_op jit(solution)/shard_map/dot_general | solution.py:40
  553.1 12.1 %copy.9 = f32[512,5376]{1,0:T(8,128)} copy(f32[512,5376]{0,1:T(8,128)} %select_bitcast_fusion) | data formatting | bytes 22020096 | tf_op jit(solution)/shard_map/jit(_where)/select_n | solution.py:46
  565.2 25.6 %scatter_fusion.1 = f32[512,5376]{1,0:T(8,128)} fusion(f32[512,5376]{1,0:T(8,128)} %scatter_fusion, s32[512]{0:T(512)S(1)} %bitcast.49, f32[512,5376]{1,0:T(8,128)} %copy.9), kind=kCustom, calls=%fused_computation.7 | custom fusion | flops 2752512 | bytes 33032192 | tf_op jit(solution)/shard_map/scatter-add | solution.py:46
  (30 shorter events, 0.8 us)
Async XLA Ops:
  6.5 9.8 %copy-start = (bf16[512,1024]{1,0:T(8,128)(2,1)S(1)}, bf16[512,1024]{1,0:T(8,128)(2,1)}, u32[]{:S(2)}) copy-start(bf16[512,1024]{1,0:T(8,128)(2,1)} %param.5) | copy-start | bytes 3145732
  6.5 9.2 %copy-start.7 = (s32[2,512]{1,0:T(2,128)S(1)}, s32[2,512]{1,0:T(2,128)}, u32[]{:S(2)}) copy-start(s32[2,512]{1,0:T(2,128)} %param.8) | copy-start | bytes 12292
  6.5 79.9 %all-reduce.3.cloned.1.call-start = ((), (), s32[]{:S(2)}) async-start(), calls=%async_computation.6 | async-start | bytes 4194304 | tf_op jit(solution)/shard_map/psum | solution.py:29
  15.8 0.6 copy-start.5
  15.8 6.3 %copy-start.3 = (pred[512]{0:T(512)(128)(4,1)}, pred[512]{0:T(512)(128)(4,1)S(1)}, u32[]{:S(2)}) copy-start(pred[512]{0:T(512)(128)(4,1)S(1)} %get-tuple-element.5) | copy-start | bytes 1540
  22.1 165.5 %reduce-scatter.3.cloned.1.call-start = ((), (), s32[]{:S(2)}) async-start(), calls=%async_computation.2 | async-start | bytes 12386304 | tf_op jit(solution)/shard_map/reduce_scatter | solution.py:38
  104.2 150.8 %all-gather.3.cloned.1.call-start = ((), (), s32[]{:S(2)}) async-start(), calls=%async_computation.3 | async-start | bytes 12386304 | tf_op jit(solution)/shard_map/all_gather | solution.py:39
  187.6 14.4 %copy-start.1 = (bf16[512,1024]{1,0:T(8,128)(2,1)S(1)}, bf16[512,1024]{1,0:T(8,128)(2,1)}, u32[]{:S(2)}) copy-start(bf16[512,1024]{1,0:T(8,128)(2,1)} %get-tuple-element.8) | copy-start | bytes 3145732
  187.6 259.3 %reduce-scatter.5.cloned.1.call-start = ((), (), s32[]{:S(2)}) async-start(), calls=%async_computation.4 | async-start | bytes 12386304 | tf_op jit(solution)/shard_map/reduce_scatter | solution.py:38
  332.2 15.4 %copy-start.4 = (pred[512]{0:T(512)(128)(4,1)S(1)}, pred[512]{0:T(512)(128)(4,1)}, u32[]{:S(2)}) copy-start(pred[512]{0:T(512)(128)(4,1)} %copy-done.3) | copy-start | bytes 1540
  362.7 151.4 %copy-start.2 = (f32[2,512,512]{2,1,0:T(8,128)S(1)}, f32[2,512,512]{2,1,0:T(8,128)}, u32[]{:S(2)}) copy-start(f32[2,512,512]{2,1,0:T(8,128)} %param.9) | copy-start | bytes 6291460
  362.7 151.4 %all-gather.5.cloned.1.call-start = ((), (), s32[]{:S(2)}) async-start(), calls=%async_computation.5 | async-start | bytes 12386304 | tf_op jit(solution)/shard_map/all_gather | solution.py:39
  553.1 12.1 %copy-start.6 = (s32[512,1]{0,1:T(1,128)S(1)}, s32[512,1]{0,1:T(1,128)}, u32[]{:S(2)}) copy-start(s32[512,1]{0,1:T(1,128)} %copy-done.5) | copy-start | bytes 6148
Sparse Core Ops, SparseCore 0:
  22.2 64.2 all-reduce.2
  104.3 83.2 reduce-scatter.2
  189.5 65.4 all-gather.2
  362.8 84.0 reduce-scatter.4
  448.6 65.4 all-gather.4
where the time goes:
time: 601 us; the launch traced here: 598 us
  waiting for transfers between devices  322 us (54%)
  matrix products  110 us (18%)
  local copies, waits for them, and re-layouts  97.5 us (16%)
  other arithmetic  55.1 us (9%)
  between operations  13.4 us (2%)
    reduce_scatter x2, waiting for transfers between devices, per_device(): lax.psum_scatter(product + local_side, 'rows', scatter_dimension=0, tiled...  167 us
    all_gather x2, waiting for transfers between devices, per_device(): negated = lax.all_gather(share, 'rows', axis=0, tiled=True)  120 us
    dot_general x2, matrix products, per_device(): jnp.dot(inverses[blk], -negated, precision=lax.Precision.HIGHEST, preferr...  78.3 us
    scatter-add x2, other arithmetic, per_device(): current.at[local_rows].add(jnp.where(inside[:, None], update, 0.0))  51.5 us
    psum x1, waiting for transfers between devices, per_device(): lax.psum(picked, 'rows').astype(jnp.float32).astype(jnp.bfloat16)  34.2 us
    dot_general x2, matrix products, per_device(): lax.dot_general(ktile, c_low, (((0,), (0,)), ((), ())), preferred_element...  31.3 us
    gather x2, local copies, waits for them, and re-layouts, per_device(): sel_coeffs = jnp.where(inside[:, None], current[local_rows], 0.0)  30.9 us
    gather x2, local copies, waits for them, and re-layouts, per_device(): targets[local_rows].astype(jnp.float32)  28.6 us
  transfers between devices with their start and end apart: 5, of which 5 were waited for; matrix products, arithmetic and copies ran while one was open for 7% of the time, Pallas kernels for 0%

commit v1 on v0

v1 whole, which is shorter than its diff:
```python
import jax
import jax.numpy as jnp
from jax import lax
from jax.sharding import PartitionSpec as P

ridge_weight = 0.5
bf16 = jnp.bfloat16
f32 = jnp.float32


def dot_nn(a, b, **kw):
    return lax.dot_general(a, b, (((1,), (0,)), ((), ())), preferred_element_type=f32, **kw)


def dot_nt(a, b, **kw):
    return lax.dot_general(a, b, (((1,), (1,)), ((), ())), preferred_element_type=f32, **kw)


def square_sums(pts):
    return jnp.sum(jnp.square(pts.astype(f32)), axis=1)


def kernel_tile(left, right):
    inner_prod = dot_nt(left, right)
    sq_dist = jnp.maximum(
        square_sums(left)[:, None] + square_sums(right)[None, :] - 2.0 * inner_prod, 0.0
    )
    return jnp.exp(-(2.0 / left.shape[1]) * sq_dist).astype(bf16)


def split_bf16(x):
    high = x.astype(bf16)
    return high, (x - high.astype(f32)).astype(bf16)


def general_path(points, targets, coeffs, block_ids, inverses):
    rows_here = points.shape[0]
    first_row = lax.axis_index("rows") * rows_here
    zero_low = jnp.zeros((), bf16)
    current = coeffs
    for blk in range(2):
        local_ids = block_ids[blk] - first_row
        inside = (local_ids >= 0) & (local_ids < rows_here)
        local_rows = jnp.clip(local_ids, 0, rows_here - 1)
        picked = jnp.where(inside[:, None], points[local_rows], zero_low)
        block_pts = lax.psum(picked, "rows").astype(f32).astype(bf16)
        ktile = kernel_tile(points, block_pts)
        c_low = current.astype(bf16)
        sel_targets = jnp.where(inside[:, None], targets[local_rows].astype(f32), 0.0)
        sel_coeffs = jnp.where(inside[:, None], current[local_rows], 0.0)
        local_side = ridge_weight * sel_coeffs - sel_targets
        product = lax.dot_general(
            ktile, c_low, (((0,), (0,)), ((), ())), preferred_element_type=f32
        )
        share = lax.psum_scatter(product + local_side, "rows", scatter_dimension=0, tiled=True)
        negated = lax.all_gather(share, "rows", axis=0, tiled=True)
        update = jnp.dot(
            inverses[blk], -negated, precision=lax.Precision.HIGHEST, preferred_element_type=f32
        )
        current = current.at[local_rows].add(jnp.where(inside[:, None], update, 0.0))
    return current


def solution(mesh):
    n = mesh.shape["rows"]
    chips = n // 2
    bits = chips.bit_length() - 1
    ring = [k ^ (k >> 1) for k in range(chips)]
    place = [ring.index(k) for k in range(chips)]

    def core_perm(chip_of):
        return [(i, 2 * chip_of(i // 2, i % 2) + i % 2) for i in range(n)]

    sib_perm = [(i, i ^ 1) for i in range(n)]
    ring_perm = core_perm(
        lambda chip, core: ring[(place[chip] + (1 if core == 0 else chips - 1)) % chips]
    )

    def stage_bit(stage, core):
        return 1 << (stage if core == 0 else bits - 1 - stage)

    def to_sib(x):
        return lax.ppermute(x, "rows", sib_perm)

    def owners(ids, rows_here):
        return ids // (2 * rows_here)

    def spread_enough(block_ids, rows_here):
        total = block_ids.size
        own = owners(block_ids.reshape(total), rows_here)
        counts = [jnp.sum((own == k).astype(jnp.int32)) for k in range(chips)]
        fits = jnp.bool_(True)
        for k in range(chips):
            fits &= counts[k] >= total // (2 * chips)
        for stage in range(bits):
            cap = stage_cap(total, stage)
            for core in range(2):
                done = sum(stage_bit(s, core) for s in range(stage))
                for base in range(chips):
                    if base & done:
                        continue
                    group = [k for k in range(chips) if k & ~done == base]
                    fits &= sum(counts[k] for k in group) <= cap
        return fits

    def stage_cap(total, stage):
        return min(total, total // 2 + ((1 << stage) - 1) * (total // chips))

    def spread_path(points, targets, coeffs, block_ids, inverses):
        rows_here, feats = points.shape
        cols = coeffs.shape[1]
        half = cols // 2
        half_f = feats // 2
        me = lax.axis_index("rows")
        chip, core = me // 2, me % 2
        blk_size = block_ids.shape[1]
        total = 2 * blk_size
        piece = total // (2 * chips)
        steps = 2 * chips - 1

        ids = block_ids.reshape(total)
        own = owners(ids, rows_here)
        ids_row = ids[None, :]
        index = jnp.arange(total, dtype=jnp.int32)
        my_first = me * rows_here
        sib_first = (me ^ 1) * rows_here
        within = jnp.arange(rows_here, dtype=jnp.int32)
        pt_ids = jnp.concatenate([my_first + within, sib_first + within])
        pick = (pt_ids[:, None] == ids_row).astype(bf16)

        pts_chip = jnp.concatenate([points, to_sib(points)], axis=0)
        pts_mine = lax.dynamic_slice(pts_chip, (0, core * half_f), (2 * rows_here, half_f))
        pts_other = lax.dynamic_slice(pts_chip, (0, (1 - core) * half_f), (2 * rows_here, half_f))
        pts_local = jnp.concatenate([pts_mine, pts_other], axis=1)

        def pack_matrix(member, cap):
            flags = member.astype(jnp.int32)
            before = (index[:, None] > index[None, :]).astype(jnp.int32)
            rank = jnp.sum(before * flags[None, :], axis=1)
            slot = jnp.where(member, rank, -1)
            return (jnp.arange(cap, dtype=jnp.int32)[:, None] == slot[None, :]).astype(bf16)

        block_half = dot_nn(pick.T, pts_mine).astype(bf16)
        for stage in range(bits):
            cap = stage_cap(total, stage)
            done0 = sum(stage_bit(s, 0) for s in range(stage))
            done1 = sum(stage_bit(s, 1) for s in range(stage))
            done = jnp.where(core == 0, done0, done1)
            bit = jnp.where(core == 0, stage_bit(stage, 0), stage_bit(stage, 1))
            mine = (own & ~done) == (chip & ~done)
            theirs = (own & ~done) == ((chip ^ bit) & ~done)
            sent = dot_nn(pack_matrix(mine, cap), block_half).astype(bf16)
            got = lax.ppermute(
                sent, "rows", core_perm(lambda k, c, s=stage: k ^ stage_bit(s, c))
            )
            unpacked = lax.dot_general(
                pack_matrix(theirs, cap), got, (((0,), (0,)), ((), ())), preferred_element_type=f32
            )
            block_half = (block_half.astype(f32) + unpacked).astype(bf16)
        block_pts = jnp.concatenate([block_half, to_sib(block_half)], axis=1)

        c_low = coeffs.astype(bf16)
        mine_at, other_at = core * half, (1 - core) * half

        def cut(x, at):
            return lax.dynamic_slice(x, (0, at), (rows_here, half))

        moved = jnp.concatenate(
            [
                cut(c_low, mine_at),
                to_sib(cut(c_low, other_at)),
                cut(targets, mine_at),
                to_sib(cut(targets, other_at)),
            ],
            axis=0,
        )

        ktile = kernel_tile(pts_local, block_pts)
        against = (ktile.astype(f32) + ridge_weight * pick.astype(f32)).astype(bf16)
        left = jnp.concatenate([-against, pick], axis=0)
        cross = kernel_tile(block_pts[blk_size:], block_pts[:blk_size]).astype(f32)
        cross += ridge_weight * (ids[blk_size:, None] == ids[None, :blk_size]).astype(f32)
        exact = dict(precision=lax.Precision.HIGHEST)
        lower = -dot_nn(inverses[1], dot_nn(cross, inverses[0], **exact), **exact)
        inv_map = jnp.concatenate(
            [
                jnp.concatenate([inverses[0], jnp.zeros_like(lower)], axis=1),
                jnp.concatenate([lower, inverses[1]], axis=1),
            ],
            axis=0,
        )

        norms = square_sums(block_pts)
        bell = jnp.exp((2.0 / feats) * (jnp.min(norms) - norms))
        along = []
        for blk in range(2):
            part = slice(blk * blk_size, (blk + 1) * blk_size)
            way = jnp.sum(inverses[blk] * bell[None, part], axis=1)
            way = way * lax.rsqrt(jnp.maximum(jnp.sum(way * way), 1e-30))
            along.append(jnp.pad(way, (blk * blk_size, (1 - blk) * blk_size)))
        rows_along = dot_nn(jnp.stack(along), inv_map, **exact)
        rest_map = inv_map - sum(along[b][:, None] * rows_along[b][None, :] for b in range(2))
        map_high, map_low = split_bf16(rest_map)
        coarse, fine = split_bf16(rows_along)
        weigh = dot_nt(jnp.concatenate([coarse, fine], axis=0), left)
        weigh = weigh[:2] + weigh[2:]
        weigh = jnp.concatenate(split_bf16(weigh), axis=0)
        amount = dot_nn(weigh, moved)
        amount = amount[:2] + amount[2:]
        for stage in range(bits):
            amount = amount + lax.ppermute(
                amount, "rows", core_perm(lambda k, c, s=stage: k ^ stage_bit(s, c))
            )
        amount_sib = to_sib(amount)

        def ring_place(which):
            return sum(jnp.where(which == k, place[k], 0) for k in range(chips))

        ahead = ring_place(own) - ring_place(chip)
        ahead = jnp.where(core == 0, -ahead, ahead)
        key = (ahead + 2 * chips - 1) % chips
        key = key * total + index
        position = jnp.sum((key[None, :] < key[:, None]).astype(jnp.int32), axis=1)
        order = (index[:, None] == position[None, :]).astype(bf16)
        row_ids = jnp.sum(jnp.where(index[:, None] == position[None, :], ids_row, 0), axis=1)
        lag = jnp.sum((key // total == 0).astype(jnp.int32))

        def shares(lo, hi):
            mat = order[lo * piece : hi * piece]
            high = dot_nn(mat, map_high).astype(bf16)
            low = dot_nn(mat, map_low).astype(bf16)
            weights = (dot_nt(high, left) + dot_nt(low, left)).astype(bf16)
            return dot_nn(weights, moved)

        cuts = [0, 1, chips, 2 * chips]
        share = []
        for lo, hi in zip(cuts[:-1], cuts[1:]):
            group = shares(lo, hi)
            share += [group[k * piece : (k + 1) * piece] for k in range(hi - lo)]

        tiles = max(1, half // 128)
        first = (tiles + 1) // 2 * 128
        bands = [(0, first), (first, half)] if first < half else [(0, half)]
        arrived = [[] for _ in bands]
        final = [[None] * (steps + 1) for _ in bands]
        spot = jnp.arange(piece, dtype=jnp.int32)
        for step in range(steps + 1):
            for b, (lo, hi) in enumerate(bands):
                value = share[step][:, lo:hi]
                if step > 0:
                    source = step * piece + spot - lag
                    slots = jnp.arange(step * piece, dtype=jnp.int32)
                    shift = (source[:, None] == slots[None, :]).astype(bf16)
                    value = value + dot_nn(shift, jnp.concatenate(arrived[b], axis=0))
                final[b][step] = value
                if step < steps:
                    arrived[b].append(lax.ppermute(value.astype(bf16), "rows", ring_perm))

        start = chips - 1
        result = coeffs
        parts = []
        for step in range(start, steps + 1):
            whole = jnp.concatenate([final[b][step] for b in range(len(bands))], axis=1)
            parts.append(split_bf16(whole))
        mine = jnp.concatenate([p for part in parts for p in part], axis=0)
        theirs = jnp.concatenate([to_sib(p) for part in parts for p in part], axis=0)
        spots = jnp.concatenate(
            [row_ids[s * piece : (s + 1) * piece] for s in range(start, steps + 1) for _ in range(2)]
        )
        place_rows = ((my_first + within)[:, None] == spots[None, :]).astype(bf16)
        mine_new = dot_nn(place_rows, mine)
        theirs_new = dot_nn(place_rows, theirs)
        here = (my_first + within)[:, None] == ids_row
        for b in range(2):
            scale = jnp.sum(jnp.where(here, along[b][None, :], 0.0), axis=1)[:, None]
            mine_new = mine_new + scale * amount[b][None, :]
            theirs_new = theirs_new + scale * amount_sib[b][None, :]
        low_half = jnp.where(core == 0, mine_new, theirs_new)
        high_half = jnp.where(core == 0, theirs_new, mine_new)
        return result + jnp.concatenate([low_half, high_half], axis=1)

    def per_device(points, targets, coeffs, block_ids, inverses):
        return lax.cond(
            spread_enough(block_ids, points.shape[0]),
            spread_path,
            general_path,
            points,
            targets,
            coeffs,
            block_ids,
            inverses,
        )

    return jax.shard_map(
        per_device,
        mesh=mesh,
        in_specs=(P("rows", None), P("rows", "labels"), P("rows", "labels"), P(), P()),
        out_specs=P("rows", "labels"),
        check_vma=False,
    )
```

time: 601 us -> 302 us (0.50)
  waiting for transfers between devices: 322 us -> 39.2 us
  local copies, waits for them, and re-layouts: 97.5 us -> 32.9 us
  starting transfers between devices: 0.34 us -> 30.9 us
  other arithmetic: 55.1 us -> 36.7 us
  matrix products: 110 us -> 125 us
  loops' own time: 0 us -> 10.1 us
  between operations: 13.4 us -> 23.3 us
    reduce_scatter x2 -> x0, waiting for transfers between devices: 167 us -> none  [per_device(): lax.psum_scatter(product + local_side, 'rows', scatter_dimension=0, tiled...]
    all_gather x2 -> x0, waiting for transfers between devices: 120 us -> none  [per_device(): negated = lax.all_gather(share, 'rows', axis=0, tiled=True)]
    gather x6 -> x0, local copies, waits for them, and re-layouts: 63.5 us -> none  [the longest x2 30.9 us: per_device(): sel_coeffs = jnp.where(inside[:, None], current[local_rows], 0.0)]
    scatter-add x2 -> x0, other arithmetic: 51.5 us -> none  [per_device(): current.at[local_rows].add(jnp.where(inside[:, None], update, 0.0))]
    ppermute x0 -> x33, waiting for transfers between devices: none -> 39.2 us  [the longest x14 24.6 us: spread_path(): arrived[b].append(lax.ppermute(value.astype(bf16), 'rows', ring_perm))]
    psum x1 -> x0, waiting for transfers between devices: 34.2 us -> none  [per_device(): lax.psum(picked, 'rows').astype(jnp.float32).astype(jnp.bfloat16)]
    ppermute x0 -> x33, starting transfers between devices: none -> 30.9 us  [the longest x14 18.6 us: spread_path(): arrived[b].append(lax.ppermute(value.astype(bf16), 'rows', ring_perm))]
    select_n x2 -> x0, local copies, waits for them, and re-layouts: 24.2 us -> none  [per_device(): jnp.where(inside[:, None], update, 0.0)]
  transfers between devices with their start and end apart: 5 -> 33, of which waited for: 5 -> 16; matrix products, arithmetic and copies ran while one was open for 7% -> 53% of each run, Pallas kernels for 0% -> 0%
where the time goes in v1:
time: 302 us; the launch traced here: 298 us
  matrix products  125 us (41%)
  waiting for transfers between devices  39.2 us (13%)
  other arithmetic  36.7 us (12%)
  local copies, waits for them, and re-layouts  32.9 us (11%)
  starting transfers between devices  30.9 us (10%)
  between operations  23.3 us (8%)
  loops' own time  10.1 us (3%)
    dot_general x28, matrix products, dot_nn(): lax.dot_general(a, b, (((1,), (0,)), ((), ())), preferred_element_type=f3...  88.1 us
    dot_general x7, matrix products, dot_nt(): lax.dot_general(a, b, (((1,), (1,)), ((), ())), preferred_element_type=f3...  35.3 us
    ppermute x14, waiting for transfers between devices, spread_path(): arrived[b].append(lax.ppermute(value.astype(bf16), 'rows', ring_perm))  24.6 us
    ppermute x14, starting transfers between devices, spread_path(): arrived[b].append(lax.ppermute(value.astype(bf16), 'rows', ring_perm))  18.6 us
    ppermute x2, waiting for transfers between devices, spread_path(): lax.ppermute(sent, 'rows', core_perm(lambda k, c, s=stage: k ^ stage_bit(...  13.5 us
    another operation x1, loops' own time, per_device(): lax.cond(spread_enough(block_ids, points.shape[0]), spread_path, general_...  10.1 us
    unnamed x7, local copies, waits for them, and re-layouts  9.26 us
    dynamic_slice x2, local copies, waits for them, and re-layouts, cut(): return lax.dynamic_slice(x, (0, at), (rows_here, half))  8.4 us
  transfers between devices with their start and end apart: 33, of which 16 were waited for; matrix products, arithmetic and copies ran while one was open for 53% of the time, Pallas kernels for 0%

profile of v1, /device:TPU:0, one launch (start us, length us, event | category | flops | bytes accessed | tf_op | source)
XLA Modules:
  0.0 298.4 jit_solution(9770406023424744258)
XLA Ops:
  6.5 9.2 %copy.81 = f32[512,5376]{1,0:T(8,128)} copy(f32[512,5376]{1,0:T(8,128)} %param.9) | data formatting | bytes 22020096
  26.2 265.1 %conditional.1 = (f32[512,5376]{1,0:T(8,128)}) conditional(s32[]{:T(128)} %convert_element_type.314, (s32[2,512]{1,0:T(2,128)S(1)}, bf16[512,1024]{1,0:T(8,128)(2,1)S(1)}, f32[512,5376]{1,0:T(8,128)}, bf16[512,5376]{1,0:T(8,128)(2,1)}, f32[2,512,512]{2,1,0:T(8,128)S(1)}) %tuple.109, (s32[2,512]{1,0:T(2,128)S(1)}, f32[2,512,512]{2,1,0:T(8,128)S(1)}, ...), branch_computations={%region_4.14_spmd, %region_14.33_spmd} | conditional | flops 43854184448 | bytes 722281344 | solution.py:283
  34.3 7.3 %convert_element_type.264 = bf16[512,5376]{1,0:T(8,128)(2,1)} convert(f32[512,5376]{1,0:T(8,128)} %get-tuple-element.33) | non-fusion elementwise | flops 2752512 | bytes 16515072 | tf_op jit(solution)/shard_map/cond/branch_1_fun/convert_element_type | solution.py:162
  41.6 5.6 %constant_dynamic-slice_fusion.3 = (bf16[512,2688]{1,0:T(8,128)(2,1)}, bf16[512,2688]{1,0:T(8,128)(2,1)}) fusion(bf16[512,5376]{1,0:T(8,128)(2,1)} %convert_element_type.264, s32[]{:T(128)S(6)} %select_n.273, s32[]{:T(128)S(6)} %select_n.274), kind=kLoop, calls=%fused_computation.360 | loop fusion | bytes 11010056 | tf_op jit(solution)/shard_map/cond/branch_1_fun/dynamic_slice | solution.py:166
  47.7 2.8 constant_dynamic-slice_fusion.1
  61.8 3.0 %collective-permute-start.1 = (bf16[512,512]{1,0:T(8,128)(2,1)S(1)}, bf16[512,512]{1,0:T(8,128)(2,1)S(1)}, u32[]{:S(2)}, u32[]{:S(2)}) collective-permute-start(bf16[512,512]{1,0:T(8,128)(2,1)S(1)} %fusion.57), channel_id=1, source_target_pairs={{0,8},{4,20},{8,0},{12,28},{16,24},{20,4},{24,16},{28,12},{1,9},{5... | collective-permute-start | bytes 1572872 | tf_op jit(solution)/shard_map/cond/branch_1_fun/ppermute | solution.py:153
  66.0 5.9 %collective-permute-done.1 = bf16[512,512]{1,0:T(8,128)(2,1)S(1)} collective-permute-done((bf16[512,512]{1,0:T(8,128)(2,1)S(1)}, bf16[512,512]{1,0:T(8,128)(2,1)S(1)}, u32[]{:S(2)}, u32[]{:S(2)}) %collective-permute-start.1) | collective-permute-done | bytes 524320 | tf_op jit(solution)/shard_map/cond/branch_1_fun/ppermute | solution.py:153
  78.3 7.6 %collective-permute-done.2 = bf16[768,512]{1,0:T(8,128)(2,1)S(1)} collective-permute-done((bf16[768,512]{1,0:T(8,128)(2,1)S(1)}, bf16[768,512]{1,0:T(8,128)(2,1)S(1)}, u32[]{:S(2)}, u32[]{:S(2)}) %collective-permute-start.2) | collective-permute-done | bytes 786464 | tf_op jit(solution)/shard_map/cond/branch_1_fun/ppermute | solution.py:153
  112.1 5.2 %fusion.14 = bf16[1024,1024]{1,0:T(8,128)(2,1)S(1)} fusion(f32[1024]{0:T(1024)S(1)} %multiply_reduce_fusion.1, f32[1024]{0:T(1024)S(1)} %multiply_reduce_fusion, bf16[1024,512]{1,0:T(8,128)(2,1)S(1)} %copy-done.6, bf16[1024,512]{1,0:T(8,128)(2,1)S(1)} %copy-done.9, bf16[1024,512]{0,1:T(8,128)(2,1)} %collective-permute-done.3, ...), kind=kOutput, calls=%fused_computation.57 | convolution fusion | flops 2170552320 | bytes 6307840 | tf_op jit(solution)/shard_map/cond/branch_1_fun/dot_general | solution.py:16
  118.6 3.0 %subtract_convert_fusion = bf16[1024,1024]{0,1:T(8,128)(2,1)} fusion(f32[1024]{0:T(1024)S(1)} %bitcast.112, f32[1024]{0:T(1024)S(1)} %pad.8, f32[1024]{0:T(1024)S(1)} %bitcast.108, f32[1024]{0:T(1024)S(1)} %pad.7, f32[512,512]{0,1:T(8,128)S(1)} %copy-done.10, f32[512,512]{0,1:T(8,128)S(1)} %fusion.44, f32[512,512]{0,1:T(8,128)S(1)} %copy-done.12), kind=kLoop, calls=%fused_computation.21 | loop fusion | flops 12582912 | bytes 5259264 | tf_op jit(solution)/shard_map/cond/branch_1_fun/convert_element_type | solution.py:33
  121.6 5.6 %fusion.60 = f32[128,2048]{1,0:T(8,128)} fusion(pred[1024,1024]{1,0:T(32,128)(4,1)} %iota_compare_fusion.2, bf16[1024,1024]{1,0:T(8,128)(2,1)} %compare_convert_fusion, bf16[1024,1024]{1,0:T(8,128)(2,1)} %copy-done.36, f32[1024]{0:T(1024)S(1)} %bitcast.113, f32[1024]{0:T(1024)S(1)} %pad.8, f32[1024]{0:T(1024)S(1)} %bitcast.109, f32[1024]{0:T(1024)S(1)} %pad.7, ...), kind=kOutput, calls=%fused_computation.120 | convolution fusion | flops 823263232 | bytes 8536064 | tf_op jit(solution)/shard_map/cond/branch_1_fun/dot_general | solution.py:16
  127.2 6.2 %fusion.11 = bf16[128,2048]{1,0:T(8,128)(2,1)} fusion(f32[128,2048]{1,0:T(8,128)} %fusion.60, bf16[1024,1024]{0,1:T(8,128)(2,1)} %subtract_convert_fusion, pred[1024,1024]{1,0:T(32,128)(4,1)} %iota_compare_fusion.2, bf16[1024,1024]{1,0:T(8,128)(2,1)} %compare_convert_fusion, bf16[1024,1024]{1,0:T(8,128)(2,1)} %copy-done.36), kind=kOutput, calls=%fused_computation.54 | convolution fusion | flops 814350336 | bytes 7995392 | tf_op jit(solution)/shard_map/cond/branch_1_fun/dot_general | solution.py:16
  133.4 3.8 %convolution_convert_fusion.1 = bf16[384,1024]{1,0:T(8,128)(2,1)} fusion(bf16[1024,1024]{0,1:T(8,128)(2,1)} %subtract_convert_fusion, pred[1024,1024]{1,0:T(32,128)(4,1)} %iota_compare_fusion.2), kind=kOutput, calls=%fused_computation.87 | convolution fusion | flops 805699584 | bytes 3276800 | tf_op jit(solution)/shard_map/cond/branch_1_fun/dot_general | solution.py:12
  139.6 7.0 %fusion.109 = f32[384,2048]{1,0:T(8,128)} fusion(pred[1024,1024]{1,0:T(32,128)(4,1)} %iota_compare_fusion.2, bf16[1024,1024]{1,0:T(8,128)(2,1)} %compare_convert_fusion, bf16[1024,1024]{1,0:T(8,128)(2,1)} %copy-done.36, f32[1024]{0:T(1024)S(1)} %bitcast.114, f32[1024]{0:T(1024)S(1)} %pad.8, f32[1024]{0:T(1024)S(1)} %bitcast.110, f32[1024]{0:T(1024)S(1)} %pad.7, ...), kind=kOutput, calls=%fused_computation.181 | convolution fusion | flops 2434138112 | bytes 10895360 | tf_op jit(solution)/shard_map/cond/branch_1_fun/dot_general | solution.py:16
  146.5 8.2 %fusion.98 = f32[512,2048]{1,0:T(8,128)} fusion(pred[1024,1024]{1,0:T(32,128)(4,1)} %iota_compare_fusion.2, bf16[1024,1024]{1,0:T(8,128)(2,1)} %compare_convert_fusion, bf16[1024,1024]{1,0:T(8,128)(2,1)} %copy-done.36, f32[1024]{0:T(1024)S(1)} %bitcast.115, f32[1024]{0:T(1024)S(1)} %pad.8, f32[1024]{0:T(1024)S(1)} %bitcast.111, f32[1024]{0:T(1024)S(1)} %pad.7, ...), kind=kOutput, calls=%fused_computation.167 | convolution fusion | flops 3239575552 | bytes 12075008 | tf_op jit(solution)/shard_map/cond/branch_1_fun/dot_general | solution.py:16
  154.7 11.4 %fusion.153 = f32[4,2688]{1,0:T(4,128)S(1)} fusion(bf16[2,2048]{1,0:T(2,128)(2,1)S(1)} %get-tuple-element.72, bf16[2,2048]{1,0:T(2,128)(2,1)S(1)} %get-tuple-element.73, bf16[512,2688]{1,0:T(8,128)(2,1)} %collective-permute-done.5, bf16[512,2688]{1,0:T(8,128)(2,1)} %get-tuple-element.102, bf16[512,2688]{1,0:T(8,128)(2,1)} %collective-permute-done.4, ...), kind=kOutput, calls=%fused_computation.284 | convolution fusion | flops 88113152 | bytes 11069440 | tf_op jit(solution)/shard_map/cond/branch_1_fun/dot_general | solution.py:12
  168.3 4.4 %convolution_convert_fusion = bf16[128,2688]{1,0:T(8,128)(2,1)S(1)} fusion(bf16[128,2048]{1,0:T(8,128)(2,1)S(1)} %copy-done.37, bf16[512,2688]{1,0:T(8,128)(2,1)} %collective-permute-done.5, bf16[512,2688]{1,0:T(8,128)(2,1)S(1)} %copy-done.17, bf16[512,2688]{1,0:T(8,128)(2,1)} %collective-permute-done.4, bf16[512,2688]{1,0:T(8,128)(2,1)S(1)} %copy-done.16), kind=kOutput, calls=%fused_computation.35 | convolution fusion | flops 1453670400 | bytes 12222464 | tf_op jit(solution)/shard_map/cond/branch_1_fun/dot_general | solution.py:12
  173.7 19.6 %fusion.87 = f32[512,2688]{1,0:T(8,128)} fusion(f32[512,2048]{1,0:T(8,128)} %fusion.98, bf16[512,1024]{1,0:T(8,128)(2,1)} %fusion.29, bf16[1024,1024]{1,0:T(8,128)(2,1)} %compare_convert_fusion, bf16[1024,1024]{1,0:T(8,128)(2,1)} %copy-done.36, bf16[512,2688]{1,0:T(8,128)(2,1)} %collective-permute-done.5, bf16[512,2688]{1,0:T(8,128)(2,1)} %get-tuple-element.102, ...), kind=kOutput, calls=%fused_computation.152 | convolution fusion | flops 7839154176 | bytes 25952256 | tf_op jit(solution)/shard_map/cond/branch_1_fun/dot_general | solution.py:12
  193.3 14.7 %fusion.88 = f32[384,2688]{1,0:T(8,128)} fusion(f32[384,2048]{1,0:T(8,128)} %fusion.109, bf16[384,1024]{1,0:T(8,128)(2,1)} %convolution_convert_fusion.1, bf16[1024,1024]{1,0:T(8,128)(2,1)} %compare_convert_fusion, bf16[1024,1024]{1,0:T(8,128)(2,1)} %copy-done.36, bf16[512,2688]{1,0:T(8,128)(2,1)} %collective-permute-done.5, ...), kind=kOutput, calls=%fused_computation.153 | convolution fusion | flops 5892472832 | bytes 23265280 | tf_op jit(solution)/shard_map/cond/branch_1_fun/dot_general | solution.py:12
  225.3 3.4 %collective-permute-done.7 = bf16[128,1408]{1,0:T(8,128)(2,1)S(1)} collective-permute-done((bf16[128,1408]{1,0:T(8,128)(2,1)S(1)}, bf16[128,1408]{1,0:T(8,128)(2,1)S(1)}, u32[]{:S(2)}, u32[]{:S(2)}) %collective-permute-start.7) | collective-permute-done | bytes 360480 | tf_op jit(solution)/shard_map/cond/branch_1_fun/ppermute | solution.py:257
  265.0 3.8 %collective-permute-done.18 = bf16[128,1408]{1,0:T(8,128)(2,1)S(1)} collective-permute-done((bf16[128,1408]{1,0:T(8,128)(2,1)S(1)}, bf16[128,1408]{1,0:T(8,128)(2,1)S(1)}, u32[]{:S(2)}, u32[]{:S(2)}) %collective-permute-start.18) | collective-permute-done | bytes 360480 | tf_op jit(solution)/shard_map/cond/branch_1_fun/ppermute | solution.py:257
  270.4 6.0 %fusion.6 = f32[512,2688]{1,0:T(8,128)} fusion(bf16[1280,2688]{1,0:T(8,128)(2,1)S(1)} %get-tuple-element.76, s32[1280]{0:T(1024)S(1)} %copy-done.33, s32[512]{0:T(512)S(1)} %get-tuple-element.182), kind=kOutput, calls=%fused_computation.38 | convolution fusion | flops 3523870720 | bytes 12393472 | tf_op jit(solution)/shard_map/cond/branch_1_fun/dot_general | solution.py:12
  276.8 7.7 %fusion.3 = (f32[512,2688]{1,0:T(8,128)S(1)}, f32[512,2688]{1,0:T(8,128)S(1)}) fusion(f32[512,2688]{1,0:T(8,128)} %fusion.6, f32[2688]{0:T(1024)} %get-tuple-element.61, f32[2688]{0:T(1024)S(1)} %get-tuple-element.60, f32[2688]{0:T(1024)S(1)} %get-tuple-element.59, f32[512]{0:T(512)} %get-tuple-element.63, f32[2688]{0:T(1024)S(1)} %get-tuple-element.58, ...), kind=kOutput, calls=%fused_computation.16 | convolution fusion | flops 3537633280 | bytes 23450624 | tf_op jit(solution)/shard_map/cond/branch_1_fun/dot_general | solution.py:12
  286.8 4.2 %copy-done = f32[512,5376]{1,0:T(8,128)} copy-done((f32[512,5376]{1,0:T(8,128)}, f32[512,5376]{1,0:T(8,128)S(1)}, u32[]{:S(2)}) %copy-start) | copy-done | bytes 11010072 | tf_op jit(solution)/shard_map/cond
  (261 shorter events, 109.2 us)
Async XLA Ops:
  33.8 23.3 %collective-permute-start = (bf16[512,1024]{1,0:T(8,128)(2,1)S(1)}, bf16[512,1024]{1,0:T(8,128)(2,1)}, u32[]{:S(2)}, u32[]{:S(2)}) collective-permute-start(bf16[512,1024]{1,0:T(8,128)(2,1)S(1)} %get-tuple-element.36), channel_id=1, source_target_pairs={{0,4},{4,0},{8,12},{12,8},{16,20},{20,16},{24,28},{28,24},{1,5},{5... | collective-permute-start | bytes 3145736 | tf_op jit(solution)/shard_map/cond/branch_1_fun/ppermute | solution.py:83
  47.2 107.5 %collective-permute-start.4 = (bf16[512,2688]{1,0:T(8,128)(2,1)}, bf16[512,2688]{1,0:T(8,128)(2,1)}, u32[]{:S(2)}, u32[]{:S(2)}) collective-permute-start(bf16[512,2688]{1,0:T(8,128)(2,1)} %get-tuple-element.101), channel_id=1, source_target_pairs={{0,4},{4,0},{8,12},{12,8},{16,20},{20,16},{24,28},{28,24},{1,5},{5... | collective-permute-start | bytes 8257544 | tf_op jit(solution)/shard_map/cond/branch_1_fun/ppermute | solution.py:83
  50.4 104.3 %collective-permute-start.5 = (bf16[512,2688]{1,0:T(8,128)(2,1)}, bf16[512,2688]{1,0:T(8,128)(2,1)}, u32[]{:S(2)}, u32[]{:S(2)}) collective-permute-start(bf16[512,2688]{1,0:T(8,128)(2,1)} %get-tuple-element.103), channel_id=1, source_target_pairs={{0,4},{4,0},{8,12},{12,8},{16,20},{20,16},{24,28},{28,24},{1,5},{5... | collective-permute-start | bytes 8257544 | tf_op jit(solution)/shard_map/cond/branch_1_fun/ppermute | solution.py:83
  61.8 10.2 %collective-permute-start.1 = (bf16[512,512]{1,0:T(8,128)(2,1)S(1)}, bf16[512,512]{1,0:T(8,128)(2,1)S(1)}, u32[]{:S(2)}, u32[]{:S(2)}) collective-permute-start(bf16[512,512]{1,0:T(8,128)(2,1)S(1)} %fusion.57), channel_id=1, source_target_pairs={{0,8},{4,20},{8,0},{12,28},{16,24},{20,4},{24,16},{28,12},{1,9},{5... | collective-permute-start | bytes 1572872 | tf_op jit(solution)/shard_map/cond/branch_1_fun/ppermute | solution.py:153
  73.8 12.1 %collective-permute-start.2 = (bf16[768,512]{1,0:T(8,128)(2,1)S(1)}, bf16[768,512]{1,0:T(8,128)(2,1)S(1)}, u32[]{:S(2)}, u32[]{:S(2)}) collective-permute-start(bf16[768,512]{1,0:T(8,128)(2,1)S(1)} %fusion.43), channel_id=1, source_target_pairs={{0,16},{4,12},{8,24},{12,4},{16,0},{20,28},{24,8},{28,20},{1,17},{... | collective-permute-start | bytes 2359304 | tf_op jit(solution)/shard_map/cond/branch_1_fun/ppermute | solution.py:153
  87.0 9.0 %collective-permute-start.3 = (bf16[1024,512]{0,1:T(8,128)(2,1)S(1)}, bf16[1024,512]{0,1:T(8,128)(2,1)}, u32[]{:S(2)}, u32[]{:S(2)}) collective-permute-start(bf16[1024,512]{0,1:T(8,128)(2,1)S(1)} %add_convert_fusion.3), channel_id=1, source_target_pairs={{0,4},{4,0},{8,12},{12,8},{16,20},{20,16},{24,28},{28,24},{1,5},{5... | collective-permute-start | bytes 3145736 | tf_op jit(solution)/shard_map/cond/branch_1_fun/ppermute | solution.py:83
  166.2 41.8 %collective-permute-start.20 = (f32[2,2688]{1,0:T(2,128)S(1)}, f32[2,2688]{1,0:T(2,128)S(1)}, u32[]{:S(2)}, u32[]{:S(2)}) collective-permute-start(f32[2,2688]{1,0:T(2,128)S(1)} %slice_add_fusion.14), channel_id=1, source_target_pairs={{0,8},{4,20},{8,0},{12,28},{16,24},{20,4},{24,16},{28,12},{1,9},{5... | collective-permute-start | bytes 64520 | tf_op jit(solution)/shard_map/cond/branch_1_fun/ppermute | solution.py:211
  173.6 42.2 %collective-permute-start.9 = (bf16[128,1280]{1,0:T(8,128)(2,1)S(1)}, bf16[128,1280]{1,0:T(8,128)(2,1)S(1)}, u32[]{:S(2)}, u32[]{:S(2)}) collective-permute-start(bf16[128,1280]{1,0:T(8,128)(2,1)S(1)} %slice.205), channel_id=1, source_target_pairs={{0,8},{4,20},{8,24},{12,4},{16,0},{20,28},{24,16},{28,12},{1,9},{5... | collective-permute-start | bytes 983048 | tf_op jit(solution)/shard_map/cond/branch_1_fun/ppermute | solution.py:257
  212.3 7.5 %collective-permute-start.6 = (bf16[128,1408]{1,0:T(8,128)(2,1)S(1)}, bf16[128,1408]{1,0:T(8,128)(2,1)S(1)}, u32[]{:S(2)}, u32[]{:S(2)}) collective-permute-start(bf16[128,1408]{1,0:T(8,128)(2,1)S(1)} %slice.201), channel_id=1, source_target_pairs={{0,8},{4,20},{8,24},{12,4},{16,0},{20,28},{24,16},{28,12},{1,9},{5... | collective-permute-start | bytes 1081352 | tf_op jit(solution)/shard_map/cond/branch_1_fun/ppermute | solution.py:257
  221.2 7.5 %collective-permute-start.7 = (bf16[128,1408]{1,0:T(8,128)(2,1)S(1)}, bf16[128,1408]{1,0:T(8,128)(2,1)S(1)}, u32[]{:S(2)}, u32[]{:S(2)}) collective-permute-start(bf16[128,1408]{1,0:T(8,128)(2,1)S(1)} %fusion.90), channel_id=1, source_target_pairs={{0,8},{4,20},{8,24},{12,4},{16,0},{20,28},{24,16},{28,12},{1,9},{5... | collective-permute-start | bytes 1081352 | tf_op jit(solution)/shard_map/cond/branch_1_fun/ppermute | solution.py:257
  224.6 7.6 %collective-permute-start.11 = (bf16[128,1280]{1,0:T(8,128)(2,1)S(1)}, bf16[128,1280]{1,0:T(8,128)(2,1)S(1)}, u32[]{:S(2)}, u32[]{:S(2)}) collective-permute-start(bf16[128,1280]{1,0:T(8,128)(2,1)S(1)} %fusion.100), channel_id=1, source_target_pairs={{0,8},{4,20},{8,24},{12,4},{16,0},{20,28},{24,16},{28,12},{1,9},{5... | collective-permute-start | bytes 983048 | tf_op jit(solution)/shard_map/cond/branch_1_fun/ppermute | solution.py:257
  229.0 7.5 %collective-permute-start.8 = (bf16[128,1408]{1,0:T(8,128)(2,1)S(1)}, bf16[128,1408]{1,0:T(8,128)(2,1)S(1)}, u32[]{:S(2)}, u32[]{:S(2)}) collective-permute-start(bf16[128,1408]{1,0:T(8,128)(2,1)S(1)} %fusion.89), channel_id=1, source_target_pairs={{0,8},{4,20},{8,24},{12,4},{16,0},{20,28},{24,16},{28,12},{1,9},{5... | collective-permute-start | bytes 1081352 | tf_op jit(solution)/shard_map/cond/branch_1_fun/ppermute | solution.py:257
  238.6 9.9 %collective-permute-start.22 = (bf16[128,2688]{1,0:T(8,128)(2,1)S(1)}, bf16[128,2688]{1,0:T(8,128)(2,1)S(1)}, u32[]{:S(2)}, u32[]{:S(2)}) collective-permute-start(bf16[128,2688]{1,0:T(8,128)(2,1)S(1)} %get-tuple-element.116), channel_id=1, source_target_pairs={{0,4},{4,0},{8,12},{12,8},{16,20},{20,16},{24,28},{28,24},{1,5},{5... | collective-permute-start | bytes 2064392 | tf_op jit(solution)/shard_map/cond/branch_1_fun/ppermute | solution.py:83
  238.8 11.3 %collective-permute-start.23 = (bf16[128,2688]{1,0:T(8,128)(2,1)S(1)}, bf16[128,2688]{1,0:T(8,128)(2,1)S(1)}, u32[]{:S(2)}, u32[]{:S(2)}) collective-permute-start(bf16[128,2688]{1,0:T(8,128)(2,1)S(1)} %get-tuple-element.85), channel_id=1, source_target_pairs={{0,4},{4,0},{8,12},{12,8},{16,20},{20,16},{24,28},{28,24},{1,5},{5... | collective-permute-start | bytes 2064392 | tf_op jit(solution)/shard_map/cond/branch_1_fun/ppermute | solution.py:83
  240.4 7.5 %collective-permute-start.15 = (bf16[128,1280]{1,0:T(8,128)(2,1)S(1)}, bf16[128,1280]{1,0:T(8,128)(2,1)S(1)}, u32[]{:S(2)}, u32[]{:S(2)}) collective-permute-start(bf16[128,1280]{1,0:T(8,128)(2,1)S(1)} %get-tuple-element.166), channel_id=1, source_target_pairs={{0,8},{4,20},{8,24},{12,4},{16,0},{20,28},{24,16},{28,12},{1,9},{5... | collective-permute-start | bytes 983048 | tf_op jit(solution)/shard_map/cond/branch_1_fun/ppermute | solution.py:257
  244.8 7.7 %collective-permute-start.14 = (bf16[128,1408]{1,0:T(8,128)(2,1)S(1)}, bf16[128,1408]{1,0:T(8,128)(2,1)S(1)}, u32[]{:S(2)}, u32[]{:S(2)}) collective-permute-start(bf16[128,1408]{1,0:T(8,128)(2,1)S(1)} %get-tuple-element.174), channel_id=1, source_target_pairs={{0,8},{4,20},{8,24},{12,4},{16,0},{20,28},{24,16},{28,12},{1,9},{5... | collective-permute-start | bytes 1081352 | tf_op jit(solution)/shard_map/cond/branch_1_fun/ppermute | solution.py:257
  246.7 9.8 %collective-permute-start.24 = (bf16[128,2688]{1,0:T(8,128)(2,1)S(1)}, bf16[128,2688]{1,0:T(8,128)(2,1)S(1)}, u32[]{:S(2)}, u32[]{:S(2)}) collective-permute-start(bf16[128,2688]{1,0:T(8,128)(2,1)S(1)} %get-tuple-element.114), channel_id=1, source_target_pairs={{0,4},{4,0},{8,12},{12,8},{16,20},{20,16},{24,28},{28,24},{1,5},{5... | collective-permute-start | bytes 2064392 | tf_op jit(solution)/shard_map/cond/branch_1_fun/ppermute | solution.py:83
  247.9 10.3 %collective-permute-start.25 = (bf16[128,2688]{1,0:T(8,128)(2,1)S(1)}, bf16[128,2688]{1,0:T(8,128)(2,1)S(1)}, u32[]{:S(2)}, u32[]{:S(2)}) collective-permute-start(bf16[128,2688]{1,0:T(8,128)(2,1)S(1)} %get-tuple-element.83), channel_id=1, source_target_pairs={{0,4},{4,0},{8,12},{12,8},{16,20},{20,16},{24,28},{28,24},{1,5},{5... | collective-permute-start | bytes 2064392 | tf_op jit(solution)/shard_map/cond/branch_1_fun/ppermute | solution.py:83
  248.5 7.6 %collective-permute-start.17 = (bf16[128,1280]{1,0:T(8,128)(2,1)S(1)}, bf16[128,1280]{1,0:T(8,128)(2,1)S(1)}, u32[]{:S(2)}, u32[]{:S(2)}) collective-permute-start(bf16[128,1280]{1,0:T(8,128)(2,1)S(1)} %get-tuple-element.168), channel_id=1, source_target_pairs={{0,8},{4,20},{8,24},{12,4},{16,0},{20,28},{24,16},{28,12},{1,9},{5... | collective-permute-start | bytes 983048 | tf_op jit(solution)/shard_map/cond/branch_1_fun/ppermute | solution.py:257
  254.9 9.9 %collective-permute-start.26 = (bf16[128,2688]{1,0:T(8,128)(2,1)S(1)}, bf16[128,2688]{1,0:T(8,128)(2,1)S(1)}, u32[]{:S(2)}, u32[]{:S(2)}) collective-permute-start(bf16[128,2688]{1,0:T(8,128)(2,1)S(1)} %get-tuple-element.112), channel_id=1, source_target_pairs={{0,4},{4,0},{8,12},{12,8},{16,20},{20,16},{24,28},{28,24},{1,5},{5... | collective-permute-start | bytes 2064392 | tf_op jit(solution)/shard_map/cond/branch_1_fun/ppermute | solution.py:83
  256.0 8.9 %collective-permute-start.27 = (bf16[128,2688]{1,0:T(8,128)(2,1)S(1)}, bf16[128,2688]{1,0:T(8,128)(2,1)S(1)}, u32[]{:S(2)}, u32[]{:S(2)}) collective-permute-start(bf16[128,2688]{1,0:T(8,128)(2,1)S(1)} %get-tuple-element.81), channel_id=1, source_target_pairs={{0,4},{4,0},{8,12},{12,8},{16,20},{20,16},{24,28},{28,24},{1,5},{5... | collective-permute-start | bytes 2064392 | tf_op jit(solution)/shard_map/cond/branch_1_fun/ppermute | solution.py:83
  256.6 7.6 %collective-permute-start.19 = (bf16[128,1280]{1,0:T(8,128)(2,1)S(1)}, bf16[128,1280]{1,0:T(8,128)(2,1)S(1)}, u32[]{:S(2)}, u32[]{:S(2)}) collective-permute-start(bf16[128,1280]{1,0:T(8,128)(2,1)S(1)} %get-tuple-element.170), channel_id=1, source_target_pairs={{0,8},{4,20},{8,24},{12,4},{16,0},{20,28},{24,16},{28,12},{1,9},{5... | collective-permute-start | bytes 983048 | tf_op jit(solution)/shard_map/cond/branch_1_fun/ppermute | solution.py:257
  263.0 13.4 %collective-permute-start.28 = (bf16[128,2688]{1,0:T(8,128)(2,1)S(1)}, bf16[128,2688]{1,0:T(8,128)(2,1)S(1)}, u32[]{:S(2)}, u32[]{:S(2)}) collective-permute-start(bf16[128,2688]{1,0:T(8,128)(2,1)S(1)} %get-tuple-element.110), channel_id=1, source_target_pairs={{0,4},{4,0},{8,12},{12,8},{16,20},{20,16},{24,28},{28,24},{1,5},{5... | collective-permute-start | bytes 2064392 | tf_op jit(solution)/shard_map/cond/branch_1_fun/ppermute | solution.py:83
  264.2 12.3 %collective-permute-start.29 = (bf16[128,2688]{1,0:T(8,128)(2,1)S(1)}, bf16[128,2688]{1,0:T(8,128)(2,1)S(1)}, u32[]{:S(2)}, u32[]{:S(2)}) collective-permute-start(bf16[128,2688]{1,0:T(8,128)(2,1)S(1)} %get-tuple-element.79), channel_id=1, source_target_pairs={{0,4},{4,0},{8,12},{12,8},{16,20},{20,16},{24,28},{28,24},{1,5},{5... | collective-permute-start | bytes 2064392 | tf_op jit(solution)/shard_map/cond/branch_1_fun/ppermute | solution.py:83
  (48 other events, 344.1 us)
